TPU v7x, 32 devices: a whole 2x2x4 slice. The times are simulated.
32 devices in a mesh: groups: 2 (over y), box: 4 (over z), angle: 2 (over x), sub: 2 (over core).
Axes of the slice: x: 2, y: 2, z: 4, core: 2. Of those that a mesh axis runs over, the one named last changes fastest.
Arguments:
- currents: bfloat16 [2, 16, 48, 256], P(None, 'angle', ('groups', 'box')), parts along dimension 2, may hold values from -6 to 6
- near_blocks: bfloat16 [2, 192, 256, 256], P(None, ('groups', 'box', 'sub')), parts along dimension 1, may hold values from -0.375 to 0.375
- near_pairs: int32 [192, 2], P(('groups', 'box', 'sub')), parts along dimension 0, may hold values from 0 to 23, as said below
- near_count: int32 [16], P(('groups', 'box', 'sub')), parts along dimension 0, may hold values from 3 to 12, as said below
- radiation: bfloat16 [2, 48, 2, 128, 256], P(None, ('groups', 'box'), 'sub'), parts along dimension 1, may hold values from -0.375 to 0.375
- parent_of: int32 [48], P('groups'), parts along dimension 0, may hold values from 0 to 7
- octant: int32 [48], P('groups'), parts along dimension 0, may hold values from 0 to 7
- far0_src: int32 [48, 16], P(('groups', 'box')), parts along dimension 0, may hold values from 0 to 23
- far0_disp: int32 [48, 16], P(('groups', 'box')), parts along dimension 0, may hold values from 0 to 315
- far1_src: int32 [16, 8], P(('groups', 'box')), parts along dimension 0, may hold values from 0 to 7
- far1_disp: int32 [16, 8], P(('groups', 'box')), parts along dimension 0, may hold values from 0 to 315
- trans0: bfloat16 [316, 2, 128], replicated, may hold values from -1.5 to 1.5
- trans1: bfloat16 [316, 2, 256], replicated, may hold values from -2 to 2
- phases: float32 [8, 256], replicated, may hold values from -3.140625 to 3.140625
- interp: float32 [256, 128], replicated, may hold values from -0.5 to 0.5
Outputs:
- field: bfloat16 [2, 16, 48, 256], P(None, 'angle', ('groups', 'box'), 'sub'), parts along dimension 2
There are 2 independent parts, one for each index of `groups`. A program takes and returns all parts, laid end to end along the dimension named above; an argument that names none is the same for every part. Nothing has to cross between parts.
Inputs may be any that keep to these rules, and one draw needn't show every extreme that they name: `near_pairs`: slots come in blocks of 12, one block for each device of box and sub in that order; a slot's target is one of the 6 boxes of its device along box, and its source lies from the target to the target plus 6. Among live slots every unordered pair of boxes appears at most once. The first near_count[h] slots of holder h are live, the others are not used.
All inputs are finite; a program needn't handle non-finite values.
Results may differ from a plain program's by a relative error of at most 0.009.
Values may be sent and summed in bfloat16 or wider, within the bound.
A program may use at most 64 MiB of HBM per device.

v0:
```python
import jax
import jax.numpy as jnp
from jax import lax
from jax.sharding import PartitionSpec as P


def from_behind(value, axis, steps):
    count = lax.axis_size(axis)
    initial, last = (max(0, -steps), min(count, count - steps))
    return lax.ppermute(value, axis, [(source, source + steps) for source in range(initial, last)])


def complex_times(left_real, left_imag, right_real, right_imag):
    return (
        left_real * right_real - left_imag * right_imag,
        left_real * right_imag + left_imag * right_real,
    )


def complex_product(einsum_form, left_side, right_side):
    real_part = jnp.einsum(
        einsum_form, left_side[0], right_side[0], preferred_element_type=jnp.float32
    ) - jnp.einsum(einsum_form, left_side[1], right_side[1], preferred_element_type=jnp.float32)
    imag_part = jnp.einsum(
        einsum_form, left_side[0], right_side[1], preferred_element_type=jnp.float32
    ) + jnp.einsum(einsum_form, left_side[1], right_side[0], preferred_element_type=jnp.float32)
    return jnp.stack([real_part, imag_part])


def translate_rows(patterns, source_ids, kind_ids, op_table):
    listed, length = source_ids.shape
    picked = jnp.take(patterns, source_ids.reshape(-1), axis=2)
    picked = picked.reshape(patterns.shape[:2] + (listed, length, patterns.shape[3])).astype(
        jnp.float32
    )
    coefficients = jnp.take(op_table, kind_ids.reshape(-1), axis=0)
    coefficients = coefficients.reshape(listed, length, 2, op_table.shape[2]).astype(jnp.float32)
    part_real, part_imag = complex_times(
        picked[0], picked[1], coefficients[:, :, 0], coefficients[:, :, 1]
    )
    return jnp.stack([jnp.sum(part_real, axis=2), jnp.sum(part_imag, axis=2)])


def phase_rows(octant_ids, phases):
    selector = (
        octant_ids[:, None] == jnp.arange(phases.shape[0], dtype=jnp.int32)[None, :]
    ).astype(jnp.float32)
    angle_values = jnp.dot(selector, phases, precision=lax.Precision.HIGHEST)
    return (jnp.cos(angle_values), jnp.sin(angle_values))


def group_parents(lift_real, lift_imag, owner_map):
    highest = lax.Precision.HIGHEST
    parent_real = jnp.einsum("rb,abe->are", owner_map, lift_real, precision=highest)
    parent_imag = jnp.einsum("rb,abe->are", owner_map, lift_imag, precision=highest)
    return jnp.stack([parent_real, parent_imag]).astype(jnp.bfloat16)


def near_products(source_pool, local_targets, local_sources, near_blocks):
    source_rows = jnp.take(source_pool, local_sources, axis=2)
    target_rows = jnp.take(source_pool, local_targets, axis=2)
    forward = complex_product("apu,piu->api", source_rows, near_blocks)
    backward = complex_product("api,piu->apu", target_rows, near_blocks)
    return (forward, backward)


def shards(
    currents,
    near_blocks,
    near_pairs,
    near_count,
    radiation,
    parent_of,
    octant,
    far0_src,
    far0_disp,
    far1_src,
    far1_disp,
    trans0,
    trans1,
    phases,
    interp,
):
    highest = lax.Precision.HIGHEST
    box_slots = currents.shape[2]
    box_rank = lax.axis_index("box")
    own_start = box_rank * box_slots
    parents_here = far1_src.shape[0]
    own_radiation = radiation[:, :, 0]
    pattern = complex_product("sdu,asu->asd", own_radiation, currents).astype(jnp.bfloat16)
    every_pattern = lax.all_gather(pattern, "box", axis=2, tiled=True)
    field_finest = translate_rows(every_pattern, far0_src, far0_disp, trans0)
    lifted_up = jnp.einsum(
        "cabd,ed->cabe", every_pattern.astype(jnp.float32), interp, precision=highest
    )
    cosine, sine_part = phase_rows(octant, phases)
    lift_real, lift_imag = complex_times(lifted_up[0], lifted_up[1], cosine, sine_part)
    own_parents = box_rank * parents_here + jnp.arange(parents_here, dtype=jnp.int32)
    owner_map = (parent_of[None, :] == own_parents[:, None]).astype(jnp.float32)
    own_parent_pattern = group_parents(lift_real, lift_imag, owner_map)
    every_parent = lax.all_gather(own_parent_pattern, "box", axis=2, tiled=True)
    own_parent_field = translate_rows(every_parent, far1_src, far1_disp, trans1).astype(
        jnp.bfloat16
    )
    parent_field = lax.all_gather(own_parent_field, "box", axis=2, tiled=True)
    own_parent = lax.dynamic_slice_in_dim(parent_of, own_start, box_slots)
    own_octant = lax.dynamic_slice_in_dim(octant, own_start, box_slots)
    from_parent = jnp.take(parent_field, own_parent, axis=2).astype(jnp.float32)
    own_cosine, own_sine = phase_rows(own_octant, phases)
    down_real, down_imag = complex_times(from_parent[0], from_parent[1], own_cosine, -own_sine)
    descended = jnp.einsum(
        "case,ed->casd", jnp.stack([down_real, down_imag]), interp, precision=highest
    )
    box_field = (field_finest + descended).astype(jnp.bfloat16)
    received = complex_product("sdu,asd->asu", own_radiation, box_field)
    targets = near_pairs[:, 0]
    sources = near_pairs[:, 1]
    pair_slots = near_pairs.shape[0]
    live_mask = (jnp.arange(pair_slots, dtype=jnp.int32) < near_count[0]).astype(jnp.float32)
    mirrored = live_mask * (targets != sources).astype(jnp.float32)
    following = from_behind(currents, "box", -1)
    source_pool = jnp.concatenate([currents, following], axis=2)
    local_targets = targets - own_start
    local_sources = sources - own_start
    forward, backward = near_products(source_pool, local_targets, local_sources, near_blocks)
    positions = jnp.arange(source_pool.shape[2], dtype=jnp.int32)
    hit_targets = (local_targets[:, None] == positions[None, :]).astype(jnp.float32) * live_mask[
        :, None
    ]
    hit_sources = (local_sources[:, None] == positions[None, :]).astype(jnp.float32) * mirrored[
        :, None
    ]
    near_field = jnp.einsum("pb,capu->cabu", hit_targets, forward, precision=highest) + jnp.einsum(
        "pb,capu->cabu", hit_sources, backward, precision=highest
    )
    from_left = from_behind(near_field[:, :, box_slots:].astype(jnp.bfloat16), "box", 1).astype(
        jnp.float32
    )
    own_sum = near_field[:, :, :box_slots] + from_left + received
    summed = lax.psum_scatter(own_sum.astype(jnp.bfloat16), "sub", scatter_dimension=3, tiled=True)
    return summed


def solution(mesh):
    placed = (
        P(None, "angle", ("groups", "box"), None),
        P(None, ("groups", "box", "sub"), None, None),
        P(("groups", "box", "sub"), None),
        P(("groups", "box", "sub")),
        P(None, ("groups", "box"), "sub", None, None),
        P("groups"),
        P("groups"),
        P(("groups", "box"), None),
        P(("groups", "box"), None),
        P(("groups", "box"), None),
        P(("groups", "box"), None),
        P(),
        P(),
        P(),
        P(),
    )
    return jax.shard_map(
        shards,
        mesh=mesh,
        in_specs=placed,
        out_specs=P(None, "angle", ("groups", "box"), "sub"),
        check_vma=False,
    )
```

profile of v0, /device:TPU:0, one launch (start us, length us, event | category | flops | bytes accessed | tf_op | source)
XLA Modules:
  0.0 119.4 jit_solution(17735873804058657068)
XLA Ops:
  6.6 0.0 reduce-scatter.4.cloned.1.call-start
  6.6 1.4 %collective-permute-start = (bf16[2,8,6,256]{3,1,2,0:T(8,128)(2,1)}, bf16[2,8,6,256]{3,1,2,0:T(8,128)(2,1)}, u32[]{:S(2)}, u32[]{:S(2)}) collective-permute-start(bf16[2,8,6,256]{3,1,2,0:T(8,128)(2,1)} %param.17), channel_id=1, source_target_pairs={{4,0},{8,4},{12,8},{5,1},{9,5},{13,9},{6,2},{10,6},{14,10},{7,3},{... | collective-permute-start | bytes 147464 | tf_op jit(solution)/shard_map/ppermute | solution.py:10
  8.1 1.2 %fusion.63 = f32[6,8,128]{2,1,0:T(8,128)S(1)} fusion(bf16[2,6,1,128,256]{4,3,1,2,0:T(8,128)(2,1)} %bitcast.245, bf16[2,8,6,256]{3,1,2,0:T(8,128)(2,1)} %param.17), kind=kOutput, calls=%fused_computation.68 | convolution fusion | flops 3145728 | bytes 442368 | tf_op jit(solution)/shard_map/sdu,asu->asd/dot_general | solution.py:24
  9.3 1.2 %fusion.64 = f32[6,8,128]{2,1,0:T(8,128)S(1)} fusion(bf16[2,6,1,128,256]{4,3,1,2,0:T(8,128)(2,1)} %bitcast.246, bf16[2,8,6,256]{3,1,2,0:T(8,128)(2,1)} %param.17), kind=kOutput, calls=%fused_computation.69 | convolution fusion | flops 3145728 | bytes 442368 | tf_op jit(solution)/shard_map/sdu,asu->asd/dot_general | solution.py:21
  10.5 1.2 %fusion.45 = bf16[1,8,6,128]{3,1,2,0:T(8,128)(2,1)S(1)} fusion(f32[6,8,128]{2,1,0:T(8,128)S(1)} %fusion.63, bf16[2,6,1,128,256]{4,3,1,2,0:T(8,128)(2,1)} %bitcast.247, bf16[2,8,6,256]{3,1,2,0:T(8,128)(2,1)} %param.17), kind=kOutput, calls=%fused_computation.43 | convolution fusion | flops 3158016 | bytes 454656 | tf_op jit(solution)/shard_map/sdu,asu->asd/dot_general | solution.py:26
  11.7 1.2 %fusion.46 = bf16[1,8,6,128]{3,1,2,0:T(8,128)(2,1)S(1)} fusion(f32[6,8,128]{2,1,0:T(8,128)S(1)} %fusion.64, bf16[2,6,1,128,256]{4,3,1,2,0:T(8,128)(2,1)} %bitcast.248, bf16[2,8,6,256]{3,1,2,0:T(8,128)(2,1)} %param.17), kind=kOutput, calls=%fused_computation.44 | convolution fusion | flops 3158016 | bytes 454656 | tf_op jit(solution)/shard_map/sdu,asu->asd/dot_general | solution.py:23
  13.0 16.1 %all_gather.9 = bf16[2,8,24,128]{3,1,2,0:T(8,128)(2,1)S(1)} all-gather(bf16[2,8,6,128]{3,1,2,0:T(8,128)(2,1)S(1)} %pad_maximum_fusion.2), channel_id=1, replica_groups=mesh['groups'=2,'box'=4,'angle'=2,'sub'=2] {'box'}, dimensions={2}, use_global_device_ids=true | all-gather | bytes 122880 | tf_op jit(solution)/shard_map/all_gather | solution.py:91
  29.1 1.2 %fusion.73 = f32[2,8,24,256]{3,2,1,0:T(8,128)S(1)} fusion(f32[256,128]{1,0:T(8,128)} %param.31, bf16[2,8,24,128]{3,1,2,0:T(8,128)(2,1)S(1)} %all_gather.9), kind=kOutput, calls=%fused_computation.85 | convolution fusion | flops 150994944 | bytes 622592 | tf_op jit(solution)/shard_map/cabd,ed->cabe/dot_general | solution.py:93
  30.4 1.0 fusion.129
  31.4 0.9 fusion.47
  32.3 0.9 fusion.48
  33.2 0.1 reshape.207
  33.3 0.1 reshape.208
  33.4 0.6 compare_and_fusion.6
  33.9 0.1 dynamic_slice.7
  34.0 0.1 reshape.205
  34.1 0.1 reshape.206
  34.3 13.1 %all_gather.10 = bf16[2,8,8,256]{3,1,0,2:T(8,128)(2,1)S(1)} all-gather(bf16[2,8,2,256]{3,1,0,2:T(8,128)(2,1)S(1)} %copy.70), channel_id=1, replica_groups=mesh['groups'=2,'box'=4,'angle'=2,'sub'=2] {'box'}, dimensions={2}, use_global_device_ids=true | all-gather | bytes 81920 | tf_op jit(solution)/shard_map/all_gather | solution.py:101
  47.5 0.6 gather_fusion.3
  48.1 0.1 fusion.96
  48.2 0.6 gather_fusion.2
  48.8 0.1 select_convert_fusion.1
  49.0 13.9 %all_gather.11 = bf16[2,8,8,256]{3,1,2,0:T(8,128)(2,1)} all-gather(bf16[2,8,2,256]{3,1,2,0:T(8,128)(2,1)S(1)} %pad_maximum_fusion.4), channel_id=1, replica_groups=mesh['groups'=2,'box'=4,'angle'=2,'sub'=2] {'box'}, dimensions={2}, use_global_device_ids=true | all-gather | bytes 81920 | tf_op jit(solution)/shard_map/all_gather | solution.py:105
  62.9 0.2 fusion.130
  63.2 1.5 %gather_fusion = bf16[96,2,8,128]{3,2,1,0:T(8,128)(2,1)} fusion(bf16[2,8,24,128]{3,1,2,0:T(8,128)(2,1)S(1)} %all_gather.9, s32[1024]{0:T(1024)S(1)} %pad_clamp_fusion.4), kind=kCustom, calls=%fused_computation.2 | custom fusion | bytes 786816 | tf_op jit(solution)/shard_map/jit(_take)/gather | solution.py:32
  64.6 2.4 %gather_fusion.1 = bf16[96,2,128]{2,1,0:T(2,128)(2,1)} fusion(bf16[316,2,128]{2,1,0:T(2,128)(2,1)} %param.28, s32[1024]{0:T(1024)S(1)} %get-tuple-element.32), kind=kCustom, calls=%fused_computation.3 | custom fusion | bytes 98688 | tf_op jit(solution)/shard_map/jit(_take)/gather | solution.py:36
  67.0 1.0 fusion.87
  68.0 0.7 fusion.127
  68.7 2.0 %gather_fusion.4 = bf16[6,2,8,256]{3,2,1,0:T(8,128)(2,1)} fusion(bf16[2,8,8,256]{3,1,2,0:T(8,128)(2,1)} %all_gather.11, s32[1024]{0:T(1024)S(1)} %pad_clamp_fusion), kind=kCustom, calls=%fused_computation.6 | custom fusion | bytes 98328 | tf_op jit(solution)/shard_map/jit(_take)/gather | solution.py:108
  70.7 1.0 convert_bitcast_fusion
  71.6 1.2 select_convert_fusion
  72.8 0.9 subtract_reduce_fusion
  73.8 1.2 fusion.42
  74.9 1.2 fusion.62
  76.1 1.8 %fusion.61 = f32[6,8,256]{2,1,0:T(8,128)} fusion(bf16[2,6,1,128,256]{4,3,1,2,0:T(8,128)(2,1)} %bitcast.250, bf16[2,8,6,128]{3,1,2,0:T(8,128)(2,1)S(1)} %fusion.42), kind=kOutput, calls=%fused_computation.66 | convolution fusion | flops 3145728 | bytes 454656 | tf_op jit(solution)/shard_map/sdu,asd->asu/dot_general | solution.py:24
  77.9 0.6 constant_dynamic-update-slice_fusion.1
  78.5 0.2 fusion.41
  78.6 0.5 compare_and_fusion.3
  79.2 0.5 copy-done.10
  80.4 0.5 fusion.115
  80.9 1.4 %constant_dynamic-update-slice_fusion = bf16[2,8,12,256]{3,1,2,0:T(8,128)(2,1)} fusion(bf16[2,8,12,256]{3,1,2,0:T(8,128)(2,1)} %constant_dynamic-update-slice_fusion.1, bf16[2,8,6,256]{3,1,2,0:T(8,128)(2,1)} %collective-permute-done), kind=kLoop, calls=%fused_computation.154 | loop fusion | bytes 98304 | tf_op jit(solution)/shard_map/concatenate | solution.py:122
  82.4 2.1 %gather_fusion.5 = bf16[12,2,8,256]{3,2,1,0:T(8,128)(2,1)} fusion(bf16[2,8,12,256]{3,1,2,0:T(8,128)(2,1)} %constant_dynamic-update-slice_fusion, s32[1024]{0:T(1024)S(1)} %pad_clamp_fusion.6), kind=kCustom, calls=%fused_computation.clone | custom fusion | bytes 196656 | tf_op jit(solution)/shard_map/jit(_take)/gather | solution.py:60
  84.5 2.1 %gather_fusion.6 = bf16[12,2,8,256]{3,2,1,0:T(8,128)(2,1)} fusion(bf16[2,8,12,256]{3,1,2,0:T(8,128)(2,1)} %constant_dynamic-update-slice_fusion, s32[1024]{0:T(1024)S(1)} %pad_clamp_fusion.5), kind=kCustom, calls=%fused_computation.1.clone | custom fusion | bytes 196656 | tf_op jit(solution)/shard_map/jit(_take)/gather | solution.py:61
  86.5 1.0 fusion.81
  87.6 0.5 fusion.6
  88.1 0.5 fusion.4
  88.6 0.3 fusion.2
  89.0 0.3 fusion
  89.3 0.5 fusion.19
  89.8 0.5 fusion.25
  90.3 0.3 fusion.31
  90.6 0.3 fusion.37
  91.0 0.4 fusion.59
  91.5 0.4 fusion.57
  91.9 0.2 fusion.65
  92.2 3.9 %collective-permute-start.1 = (bf16[2,8,6,256]{3,1,2,0:T(8,128)(2,1)S(1)}, bf16[2,8,6,256]{3,1,2,0:T(8,128)(2,1)S(1)}, u32[]{:S(2)}, u32[]{:S(2)}) collective-permute-start(bf16[2,8,6,256]{3,1,2,0:T(8,128)(2,1)S(1)} %slice.295), channel_id=1, source_target_pairs={{0,4},{4,8},{8,12},{1,5},{5,9},{9,13},{2,6},{6,10},{10,14},{3,7},{... | collective-permute-start | bytes 147464 | tf_op jit(solution)/shard_map/ppermute | solution.py:10
  96.1 0.2 fusion.40
  96.3 1.6 %collective-permute-done.1 = bf16[2,8,6,256]{3,1,2,0:T(8,128)(2,1)S(1)} collective-permute-done((bf16[2,8,6,256]{3,1,2,0:T(8,128)(2,1)S(1)}, bf16[2,8,6,256]{3,1,2,0:T(8,128)(2,1)S(1)}, u32[]{:S(2)}, u32[]{:S(2)}) %collective-permute-start.1) | collective-permute-done | bytes 49184 | tf_op jit(solution)/shard_map/ppermute | solution.py:10
  97.9 1.0 copy.79
  98.9 1.7 %reshape.276 = bf16[256,96]{1,0:T(8,128)(2,1)} reshape(bf16[256,2,8,6]{3,2,1,0:T(8,128)(2,1)S(1)} %bitcast.253) | data formatting | bytes 98304
  100.6 0.0 reduce-scatter.4.cloned.1.call-update
  100.7 9.4 %reduce-scatter.4.cloned.1.call-done = bf16[128,96]{1,0:T(8,128)(2,1)} async-done(((bf16[256,96]{1,0:T(8,128)(2,1)}), bf16[128,96]{1,0:T(8,128)(2,1)}) %reduce-scatter.4.cloned.1.call-update) | async-done | bytes 24592
  110.1 1.4 %reshape.277 = bf16[128,2,8,6]{3,2,1,0:T(8,128)(2,1)S(1)} reshape(bf16[128,96]{1,0:T(8,128)(2,1)} %reduce-scatter.4.cloned.1.call-done) | data formatting | bytes 49152
  111.4 1.1 copy.75
  (70 shorter events, 0.4 us)
Async XLA Ops:
  6.5 40.9 %copy-start = (bf16[316,2,256]{2,1,0:T(2,128)(2,1)S(1)}, bf16[316,2,256]{2,1,0:T(2,128)(2,1)}, u32[]{:S(2)}) copy-start(bf16[316,2,256]{2,1,0:T(2,128)(2,1)} %param.29) | copy-start | bytes 970756
  6.5 27.4 %copy-start.18 = (s32[24]{0:T(128)S(1)}, s32[24]{0:T(128)}, u32[]{:S(2)}) copy-start(s32[24]{0:T(128)} %param.23) | copy-start | bytes 292
  6.5 56.3 %copy-start.15 = (f32[8,256]{1,0:T(8,128)S(1)}, f32[8,256]{1,0:T(8,128)}, u32[]{:S(2)}) copy-start(f32[8,256]{1,0:T(8,128)} %param.30) | copy-start | bytes 24580
  6.5 26.8 %copy-start.8 = (s32[24]{0:T(128)S(1)}, s32[24]{0:T(128)}, u32[]{:S(2)}) copy-start(s32[24]{0:T(128)} %param.22) | copy-start | bytes 292
  6.5 26.6 %copy-start.16 = (s32[2,8]{1,0:T(2,128)S(1)}, s32[2,8]{1,0:T(2,128)}, u32[]{:S(2)}) copy-start(s32[2,8]{1,0:T(2,128)} %param.26) | copy-start | bytes 196
  6.5 26.7 %copy-start.17 = (s32[2,8]{1,0:T(2,128)S(1)}, s32[2,8]{1,0:T(2,128)}, u32[]{:S(2)}) copy-start(s32[2,8]{1,0:T(2,128)} %param.27) | copy-start | bytes 196
  6.6 27.5 %copy-start.6 = (s32[6,16]{1,0:T(8,128)S(1)}, s32[6,16]{1,0:T(8,128)}, u32[]{:S(2)}) copy-start(s32[6,16]{1,0:T(8,128)} %param.24) | copy-start | bytes 1156
  6.6 27.5 %copy-start.7 = (s32[6,16]{1,0:T(8,128)S(1)}, s32[6,16]{1,0:T(8,128)}, u32[]{:S(2)}) copy-start(s32[6,16]{1,0:T(8,128)} %param.25) | copy-start | bytes 1156
  6.6 103.5 %reduce-scatter.4.cloned.1.call-start = ((), (), s32[]{:S(2)}) async-start(), calls=%async_computation.1 | async-start | bytes 98304
  6.6 74.3 %collective-permute-start = (bf16[2,8,6,256]{3,1,2,0:T(8,128)(2,1)}, bf16[2,8,6,256]{3,1,2,0:T(8,128)(2,1)}, u32[]{:S(2)}, u32[]{:S(2)}) collective-permute-start(bf16[2,8,6,256]{3,1,2,0:T(8,128)(2,1)} %param.17), channel_id=1, source_target_pairs={{4,0},{8,4},{12,8},{5,1},{9,5},{13,9},{6,2},{10,6},{14,10},{7,3},{... | collective-permute-start | bytes 147464 | tf_op jit(solution)/shard_map/ppermute | solution.py:10
  48.2 29.7 %copy-start.4 = (bf16[2,8,6,256]{3,1,2,0:T(8,128)(2,1)S(1)}, bf16[2,8,6,256]{3,1,2,0:T(8,128)(2,1)}, u32[]{:S(2)}) copy-start(bf16[2,8,6,256]{3,1,2,0:T(8,128)(2,1)} %param.17) | copy-start | bytes 147460
  48.9 29.7 %copy-start.9 = (s32[12,2]{0,1:T(2,128)S(1)}, s32[12,2]{0,1:T(2,128)}, u32[]{:S(2)}) copy-start(s32[12,2]{0,1:T(2,128)} %param.19) | copy-start | bytes 292
  64.6 23.0 %copy-start.1 = (bf16[2,12,256,256]{3,2,1,0:T(8,128)(2,1)S(1)}, bf16[2,12,256,256]{3,2,1,0:T(8,128)(2,1)}, u32[]{:S(2)}) copy-start(bf16[2,12,256,256]{3,2,1,0:T(8,128)(2,1)} %param.18) | copy-start | bytes 9437188
  70.7 7.8 %copy-start.2 = (bf16[2,6,1,128,256]{4,3,2,1,0:T(8,128)(2,1)S(1)}, bf16[2,6,1,128,256]{4,3,2,1,0:T(8,128)(2,1)}, u32[]{:S(2)}) copy-start(bf16[2,6,1,128,256]{4,3,2,1,0:T(8,128)(2,1)} %param.21) | copy-start | bytes 2359300
  79.2 0.5 copy-start.10
  79.2 0.6 copy-start.12
  89.8 1.2 %copy-start.13 = (s32[12]{0:T(128)S(1)}, s32[12]{0:T(128)}, u32[]{:S(2)}) copy-start(s32[12]{0:T(128)} %copy-done.12) | copy-start | bytes 148
  89.8 1.7 %copy-start.11 = (s32[12]{0:T(128)S(1)}, s32[12]{0:T(128)}, u32[]{:S(2)}) copy-start(s32[12]{0:T(128)} %copy-done.10) | copy-start | bytes 148
  89.8 1.7 %copy-start.14 = (f32[12]{0:T(128)S(1)}, f32[12]{0:T(128)}, u32[]{:S(2)}) copy-start(f32[12]{0:T(128)} %fusion.115) | copy-start | bytes 148
  90.3 5.8 %copy-start.3 = (bf16[2,6,1,128,256]{4,3,2,1,0:T(8,128)(2,1)S(1)}, bf16[2,6,1,128,256]{4,3,2,1,0:T(8,128)(2,1)}, u32[]{:S(2)}) copy-start(bf16[2,6,1,128,256]{4,3,2,1,0:T(8,128)(2,1)} %param.21) | copy-start | bytes 2359300
  90.3 5.8 %copy-start.5 = (f32[6,8,256]{2,1,0:T(8,128)S(1)}, f32[6,8,256]{2,1,0:T(8,128)}, u32[]{:S(2)}) copy-start(f32[6,8,256]{2,1,0:T(8,128)} %fusion.61) | copy-start | bytes 147460
  92.2 5.7 %collective-permute-start.1 = (bf16[2,8,6,256]{3,1,2,0:T(8,128)(2,1)S(1)}, bf16[2,8,6,256]{3,1,2,0:T(8,128)(2,1)S(1)}, u32[]{:S(2)}, u32[]{:S(2)}) collective-permute-start(bf16[2,8,6,256]{3,1,2,0:T(8,128)(2,1)S(1)} %slice.295), channel_id=1, source_target_pairs={{0,4},{4,8},{8,12},{1,5},{5,9},{9,13},{2,6},{6,10},{10,14},{3,7},{... | collective-permute-start | bytes 147464 | tf_op jit(solution)/shard_map/ppermute | solution.py:10
Sparse Core Ops, SparseCore 0:
  100.8 9.2 reduce-scatter.3
where the time goes:
time: 120 us; the launch traced here: 119 us
  blocking collectives  43.2 us (36%)
  local copies, waits for them, and re-layouts  20.2 us (17%)
  matrix products  17.8 us (15%)
  between operations  14.5 us (12%)
  waiting for transfers between devices  11 us (9%)
  other arithmetic  7.35 us (6%)
  starting transfers between devices  5.39 us (4%)
    all_gather x1, blocking collectives, shards(): every_pattern = lax.all_gather(pattern, 'box', axis=2, tiled=True)  16.1 us
    all_gather x1, blocking collectives, shards(): parent_field = lax.all_gather(own_parent_field, 'box', axis=2, tiled=True)  13.9 us
    all_gather x1, blocking collectives, shards(): every_parent = lax.all_gather(own_parent_pattern, 'box', axis=2, tiled=True)  13.1 us
    unnamed x2, waiting for transfers between devices  9.41 us
    unnamed x44, local copies, waits for them, and re-layouts  5.35 us
    ppermute x2, starting transfers between devices, from_behind(): lax.ppermute(value, axis, [(source, source + steps) for source in range(i...  5.35 us
    dot_general x4, matrix products, complex_product(): jnp.einsum(einsum_form, left_side[0], right_side[1], preferred_element_ty...  3.83 us
    dot_general x4, matrix products, complex_product(): jnp.einsum(einsum_form, left_side[0], right_side[0], preferred_element_ty...  3.22 us
  transfers between devices with their start and end apart: 3, of which 2 were waited for; matrix products, arithmetic and copies ran while one was open for 24% of the time, Pallas kernels for 0%

commit v1 on v0

v1 whole, which is shorter than its diff:
```python
import functools

import jax
import jax.numpy as jnp
from jax import lax
from jax.experimental import pallas as pl
from jax.experimental.pallas import tpu as pltpu
from jax.sharding import PartitionSpec as P

BF16 = jnp.bfloat16
F32 = jnp.float32
MESH = pl.DeviceIdType.MESH


def turned(value):
    half = value.shape[0] // 2
    return jnp.concatenate([-value[half:], value[:half]], axis=0)


def dot(left, right, right_dim):
    return lax.dot_general(
        left, right, (((1,), (right_dim,)), ((), ())), preferred_element_type=F32
    )


def kernel(
    n,
    pairs,
    count,
    parent_of,
    octant,
    src0,
    disp0,
    src1,
    disp1,
    currents,
    near_blocks,
    radiation,
    trans0,
    trans1,
    phases,
    interp,
    out,
    staged,
    pool,
    pool_turned,
    blocks,
    rad,
    table0,
    table1,
    phase,
    cosine,
    sine,
    interp_wide,
    pattern,
    operators,
    lifted,
    parent,
    forward,
    backward,
    near_sum,
    mirror_out,
    mirror_in,
    half_out,
    half_in,
    local_sem,
    pattern_send,
    pattern_recv,
    operator_send,
    operator_recv,
    next_send,
    next_recv,
    mirror_send,
    mirror_recv,
    half_send,
    half_recv,
):
    me = lax.axis_index("box")
    sub = lax.axis_index("sub")
    slots = currents.shape[1]
    half_rows = currents.shape[2]
    rows = 2 * half_rows
    boxes = pattern.shape[0]
    parents = parent.shape[0]
    parents_here = src1.shape[0]
    slot_count = pairs.shape[1]
    own_start = me * slots

    own_pool = pool.at[pl.ds(0, slots)]
    next_pool = pool.at[pl.ds(slots, slots)]
    sources = (currents, radiation, phases, interp, trans1, near_blocks, trans0)
    targets = (staged, rad, phase, interp_wide, table1, blocks, table0)
    local = [
        pltpu.make_async_copy(a, b, local_sem.at[i])
        for i, (a, b) in enumerate(zip(sources, targets))
    ]
    for copy in local:
        copy.start()
    get_currents, get_rad, get_phase, get_interp, get_table1, get_blocks, get_table0 = local

    barrier = pltpu.get_barrier_semaphore()
    for step in range(1, n):
        pl.semaphore_signal(
            barrier, inc=1, device_id={"box": lax.rem(me + step, n)}, device_id_type=MESH
        )
    pl.semaphore_signal(barrier, inc=1, device_id={"sub": 1 - sub}, device_id_type=MESH)

    get_currents.wait()
    for b in range(slots):
        wide = jnp.concatenate([staged[0, b].astype(F32), staged[1, b].astype(F32)], axis=0)
        pool[b] = wide.astype(BF16)
        pool_turned[b] = turned(wide).astype(BF16)
    get_rad.wait()
    own_box = pl.ds(own_start, slots)
    for b in range(slots):
        pattern[own_start + b] = (
            dot(pool[b], rad[0, b, 0], 1) + dot(pool_turned[b], rad[1, b, 0], 1)
        ).astype(BF16)

    pl.semaphore_wait(barrier, n)

    pattern_copies = []
    for step in range(1, n):
        copy = pltpu.make_async_remote_copy(
            src_ref=pattern.at[own_box],
            dst_ref=pattern.at[own_box],
            send_sem=pattern_send.at[step - 1],
            recv_sem=pattern_recv.at[step - 1],
            device_id={"box": lax.rem(me + step, n)},
            device_id_type=MESH,
        )
        copy.start()
        pattern_copies.append(copy)

    next_copy = pltpu.make_async_remote_copy(
        src_ref=own_pool,
        dst_ref=next_pool,
        send_sem=next_send,
        recv_sem=next_recv,
        device_id={"box": lax.rem(me + n - 1, n)},
        device_id_type=MESH,
    )

    @pl.when(me > 0)
    def _():
        next_copy.start()

    @pl.when(me == n - 1)
    def _():
        pool[pl.ds(slots, slots)] = jnp.zeros((slots,) + pool.shape[1:], BF16)

    get_table1.wait()
    position = lax.broadcasted_iota(jnp.int32, (parents, table1.shape[2]), 0)
    own_operator = pl.ds(me * parents_here, parents_here)
    for r in range(parents_here):
        real = jnp.zeros(position.shape, F32)
        imag = jnp.zeros(position.shape, F32)
        for k in range(src1.shape[1]):
            row = table1[disp1[r, k]].astype(F32)
            hit = position == src1[r, k]
            real = real + jnp.where(hit, row[0:1], 0.0)
            imag = imag + jnp.where(hit, row[1:2], 0.0)
        operators[me * parents_here + r] = jnp.concatenate([real, imag], axis=0).astype(BF16)
    operator_copies = []
    for step in range(1, n):
        copy = pltpu.make_async_remote_copy(
            src_ref=operators.at[own_operator],
            dst_ref=operators.at[own_operator],
            send_sem=operator_send.at[step - 1],
            recv_sem=operator_recv.at[step - 1],
            device_id={"box": lax.rem(me + step, n)},
            device_id_type=MESH,
        )
        copy.start()
        operator_copies.append(copy)

    get_phase.wait()
    cosine[...] = jnp.cos(phase[...])
    sine[...] = jnp.sin(phase[...])

    @pl.when(me < n - 1)
    def _():
        next_copy.wait_recv()

    for b in range(slots, 2 * slots):
        pool_turned[b] = turned(pool[b].astype(F32)).astype(BF16)
    get_blocks.wait()

    def near_step(p, carry):
        source = jnp.clip(pairs[1, p] - own_start, 0, 2 * slots - 1)
        target = jnp.clip(pairs[0, p] - own_start, 0, slots - 1)
        forward[p] = dot(pool[source], blocks[0, p], 1) + dot(pool_turned[source], blocks[1, p], 1)
        backward[p] = dot(pool[target], blocks[0, p], 0) + dot(pool_turned[target], blocks[1, p], 0)
        return carry

    lax.fori_loop(0, slot_count, near_step, 0, unroll=True)

    def mirror_weight(p, b):
        source = pairs[1, p]
        hit = (source - own_start == b) & (source != pairs[0, p]) & (p < count[0])
        return jnp.where(hit, 1.0, 0.0).astype(F32)

    def target_weight(p, b):
        hit = (pairs[0, p] - own_start == b) & (p < count[0])
        return jnp.where(hit, 1.0, 0.0).astype(F32)

    zero = jnp.zeros(pool.shape[1:], F32)

    def mirror_box(b, carry):
        def step(p, total):
            return total + mirror_weight(p, slots + b) * backward[p]

        mirror_out[b] = lax.fori_loop(0, slot_count, step, zero, unroll=True).astype(BF16)
        return carry

    lax.fori_loop(0, slots, mirror_box, 0)
    mirror_copy = pltpu.make_async_remote_copy(
        src_ref=mirror_out,
        dst_ref=mirror_in,
        send_sem=mirror_send,
        recv_sem=mirror_recv,
        device_id={"box": lax.rem(me + 1, n)},
        device_id_type=MESH,
    )

    @pl.when(me < n - 1)
    def _():
        mirror_copy.start()

    @pl.when(me == 0)
    def _():
        mirror_in[...] = jnp.zeros(mirror_in.shape, BF16)

    def near_box(b, carry):
        def step(p, total):
            total = total + target_weight(p, b) * forward[p]
            return total + mirror_weight(p, b) * backward[p]

        near_sum[b] = lax.fori_loop(0, slot_count, step, zero, unroll=True)
        return carry

    lax.fori_loop(0, slots, near_box, 0)

    get_interp.wait()
    narrow = interp_wide[...].astype(BF16)
    for copy in pattern_copies:
        copy.wait_recv()

    def lift_box(b, carry):
        up = dot(pattern[b], narrow, 1)
        cos_row = cosine[pl.ds(octant[b], 1), :]
        sin_row = sine[pl.ds(octant[b], 1), :]
        real, imag = up[:half_rows], up[half_rows:]
        lifted[b] = jnp.concatenate(
            [real * cos_row - imag * sin_row, real * sin_row + imag * cos_row], axis=0
        )
        return carry

    def lift_some(part, carry):
        return lax.fori_loop(
            0, slots, lambda b, c: lift_box(part * slots + b, c), carry, unroll=True
        )

    lax.fori_loop(0, boxes // slots, lift_some, 0)

    def sum_parent(r, carry):
        def part_sum(part, total):
            def step(i, total):
                b = part * slots + i
                weight = jnp.where(parent_of[b] == r, 1.0, 0.0).astype(F32)
                return total + weight * lifted[b]

            return lax.fori_loop(0, slots, step, total, unroll=True)

        total = lax.fori_loop(0, boxes // slots, part_sum, zero)
        parent[r] = total.astype(BF16).astype(F32)
        return carry

    lax.fori_loop(0, parents, sum_parent, 0)

    for copy in operator_copies:
        copy.wait_recv()
    get_table0.wait()

    def far_box(b, carry):
        quarter = jnp.zeros((half_rows, pattern.shape[2]), F32)

        def translate(k, total):
            value = pattern[src0[b, k]].astype(F32)
            factor = table0[disp0[b, k]].astype(F32)
            real, imag = value[:half_rows], value[half_rows:]
            fr, fi = factor[0:1], factor[1:2]
            return (total[0] + (real * fr - imag * fi), total[1] + (real * fi + imag * fr))

        far_real, far_imag = lax.fori_loop(
            0, src0.shape[1], translate, (quarter, quarter), unroll=True
        )
        owner = parent_of[own_start + b]
        operator = operators[owner].astype(F32)
        pf_real = jnp.zeros((half_rows, parent.shape[2]), F32)
        pf_imag = jnp.zeros((half_rows, parent.shape[2]), F32)
        for s in range(parents):
            value = parent[s]
            real, imag = value[:half_rows], value[half_rows:]
            fr = operator[s : s + 1]
            fi = operator[parents + s : parents + s + 1]
            pf_real = pf_real + (real * fr - imag * fi)
            pf_imag = pf_imag + (real * fi + imag * fr)
        pf_real = pf_real.astype(BF16).astype(F32)
        pf_imag = pf_imag.astype(BF16).astype(F32)
        spot = octant[own_start + b]
        cos_row = cosine[pl.ds(spot, 1), :]
        sin_row = sine[pl.ds(spot, 1), :]
        down = jnp.concatenate(
            [pf_real * cos_row + pf_imag * sin_row, pf_imag * cos_row - pf_real * sin_row], axis=0
        ).astype(BF16)
        field = jnp.concatenate([far_real, far_imag], axis=0) + dot(down, narrow, 0)
        field = field.astype(BF16)
        wide = turned(field.astype(F32)).astype(BF16)
        near_sum[b] += dot(field, rad[0, b, 0], 0) + dot(wide, rad[1, b, 0], 0)
        return carry

    lax.fori_loop(0, slots, far_box, 0)

    @pl.when(me > 0)
    def _():
        mirror_copy.wait_recv()

    cut = out.shape[3]
    kept = []
    for b in range(slots):
        total = near_sum[b] + mirror_in[b].astype(F32)
        low, high = total[:, :cut], total[:, cut:]
        kept.append(jnp.where(sub == 0, low, high))
        half_out[b] = jnp.where(sub == 0, high, low).astype(BF16)
    half_copy = pltpu.make_async_remote_copy(
        src_ref=half_out,
        dst_ref=half_in,
        send_sem=half_send,
        recv_sem=half_recv,
        device_id={"sub": 1 - sub},
        device_id_type=MESH,
    )
    half_copy.start()
    for copy in pattern_copies + operator_copies:
        copy.wait_send()

    @pl.when(me > 0)
    def _():
        next_copy.wait_send()

    @pl.when(me < n - 1)
    def _():
        mirror_copy.wait_send()

    half_copy.wait()
    for b in range(slots):
        total = kept[b] + half_in[b].astype(F32)
        out[0, b] = total[:half_rows].astype(BF16)
        out[1, b] = total[half_rows:].astype(BF16)


def shards(
    n,
    currents,
    near_blocks,
    near_pairs,
    near_count,
    radiation,
    parent_of,
    octant,
    far0_src,
    far0_disp,
    far1_src,
    far1_disp,
    trans0,
    trans1,
    phases,
    interp,
):
    _, angles, slots, unknowns = currents.shape
    rows = 2 * angles
    boxes = parent_of.shape[0]
    parents_here = far1_src.shape[0]
    parents = n * parents_here
    fine, coarse = interp.shape[1], interp.shape[0]
    slot_count = near_pairs.shape[0]
    cut = unknowns // lax.axis_size("sub")
    per_box = jnp.transpose(currents, (0, 2, 1, 3))
    scalars = pl.BlockSpec(memory_space=pltpu.SMEM)
    away = pl.BlockSpec(memory_space=pl.ANY)
    dma = pltpu.SemaphoreType.DMA
    result = pl.pallas_call(
        functools.partial(kernel, n),
        out_shape=jax.ShapeDtypeStruct((2, slots, angles, cut), BF16),
        in_specs=[scalars] * 8 + [away] * 7,
        out_specs=pl.BlockSpec(memory_space=pltpu.VMEM),
        scratch_shapes=[
            pltpu.VMEM(per_box.shape, BF16),
            pltpu.VMEM((2 * slots, rows, unknowns), BF16),
            pltpu.VMEM((2 * slots, rows, unknowns), BF16),
            pltpu.VMEM(near_blocks.shape, BF16),
            pltpu.VMEM(radiation.shape, BF16),
            pltpu.VMEM(trans0.shape, BF16),
            pltpu.VMEM(trans1.shape, BF16),
            pltpu.VMEM(phases.shape, F32),
            pltpu.VMEM(phases.shape, F32),
            pltpu.VMEM(phases.shape, F32),
            pltpu.VMEM(interp.shape, F32),
            pltpu.VMEM((boxes, rows, fine), BF16),
            pltpu.VMEM((parents, 2 * parents, coarse), BF16),
            pltpu.VMEM((boxes, rows, coarse), F32),
            pltpu.VMEM((parents, rows, coarse), F32),
            pltpu.VMEM((slot_count, rows, unknowns), F32),
            pltpu.VMEM((slot_count, rows, unknowns), F32),
            pltpu.VMEM((slots, rows, unknowns), F32),
            pltpu.VMEM((slots, rows, unknowns), BF16),
            pltpu.VMEM((slots, rows, unknowns), BF16),
            pltpu.VMEM((slots, rows, cut), BF16),
            pltpu.VMEM((slots, rows, cut), BF16),
            dma((7,)),
            dma((n - 1,)),
            dma((n - 1,)),
            dma((n - 1,)),
            dma((n - 1,)),
            dma,
            dma,
            dma,
            dma,
            dma,
            dma,
        ],
        compiler_params=pltpu.CompilerParams(
            collective_id=0, has_side_effects=True, vmem_limit_bytes=60 * 1024 * 1024
        ),
    )(
        jnp.transpose(near_pairs),
        near_count,
        parent_of,
        octant,
        far0_src,
        far0_disp,
        far1_src,
        far1_disp,
        per_box,
        near_blocks,
        radiation,
        trans0,
        trans1,
        phases,
        interp,
    )
    return jnp.transpose(result, (0, 2, 1, 3))


def solution(mesh):
    placed = (
        P(None, "angle", ("groups", "box"), None),
        P(None, ("groups", "box", "sub"), None, None),
        P(("groups", "box", "sub"), None),
        P(("groups", "box", "sub")),
        P(None, ("groups", "box"), "sub", None, None),
        P("groups"),
        P("groups"),
        P(("groups", "box"), None),
        P(("groups", "box"), None),
        P(("groups", "box"), None),
        P(("groups", "box"), None),
        P(),
        P(),
        P(),
        P(),
    )
    return jax.shard_map(
        functools.partial(shards, mesh.shape["box"]),
        mesh=mesh,
        in_specs=placed,
        out_specs=P(None, "angle", ("groups", "box"), "sub"),
        check_vma=False,
    )
```

time: 120 us -> 19 us (0.16)
  blocking collectives: 43.2 us -> 0 us
  local copies, waits for them, and re-layouts: 20.2 us -> 1.35 us
  matrix products: 17.8 us -> 0 us
  Pallas kernels: 0 us -> 16.8 us
  between operations: 14.5 us -> 0.66 us
  waiting for transfers between devices: 11 us -> 0 us
  other arithmetic: 7.35 us -> 0 us
  starting transfers between devices: 5.39 us -> 0 us
    all_gather x3 -> x0, blocking collectives: 43.2 us -> none  [the longest x1 16.1 us: shards(): every_pattern = lax.all_gather(pattern, 'box', axis=2, tiled=True)]
    dot_general x24 -> x0, matrix products: 17.8 us -> none  [the longest x4 3.83 us: complex_product(): jnp.einsum(einsum_form, left_side[0], right_side[1], preferred_element_ty...]
    pallas_call x0 -> x1, Pallas kernels: none -> 16.8 us  [shards(): pl.pallas_call(functools.partial(kernel, n), out_shape=jax.ShapeDtypeStru...]
    gather x7 -> x0, local copies, waits for them, and re-layouts: 11.2 us -> none  [the longest x2 2.97 us: translate_rows(): coefficients = jnp.take(op_table, kind_ids.reshape(-1), axis=0)]
    unnamed x2 -> x0, waiting for transfers between devices: 9.41 us -> none
    ppermute x2 -> x0, starting transfers between devices: 5.35 us -> none  [from_behind(): lax.ppermute(value, axis, [(source, source + steps) for source in range(i...]
    unnamed x44 -> x1, local copies, waits for them, and re-layouts: 5.35 us -> 1.35 us
    convert_element_type x7 -> x0, other arithmetic: 3.29 us -> none  [the longest x2 1.26 us: translate_rows(): picked.reshape(patterns.shape[:2] + (listed, length, patterns.shape[3]))]
  transfers between devices with their start and end apart: 3 -> 0, of which waited for: 2 -> 0; matrix products, arithmetic and copies ran while one was open for 24% -> 0% of each run, Pallas kernels for 0% -> 0%
where the time goes in v1:
time: 19 us; the launch traced here: 18.8 us
  Pallas kernels  16.8 us (88%)
  local copies, waits for them, and re-layouts  1.35 us (7%)
  between operations  0.66 us (3%)
    pallas_call x1, Pallas kernels, shards(): pl.pallas_call(functools.partial(kernel, n), out_shape=jax.ShapeDtypeStru...  16.8 us
    unnamed x1, local copies, waits for them, and re-layouts  1.35 us

profile of v1, /device:TPU:0, one launch (start us, length us, event | category | flops | bytes accessed | tf_op | source)
XLA Modules:
  0.0 18.8 jit_solution(9846042113746505117)
XLA Ops:
  0.7 16.8 %shard_map.145 = bf16[2,6,8,128]{3,2,1,0:T(8,128)(2,1)} custom-call(s32[2,12]{1,0:T(2,128)} %bitcast.5, s32[1]{0:T(128)S(6)} %copy.17.count, s32[24]{0:T(128)} %parent_of.1, s32[24]{0:T(128)} %octant.1, s32[6,16]{1,0:T(8,128)} %src0.1, s32[6,16]{1,0:T(8,128)} %disp0.1, s32[2,8]{1,0:T(2,128)} %src1.1, s32[2,8]{1,0:T(2,128)} %disp1.1, ...), custom_call_target="tpu_custom_call" | custom-call | tf_op jit(solution)/shard_map/pallas_call | solution.py:393
  17.5 1.3 %copy.18 = bf16[2,8,6,128]{3,1,2,0:T(8,128)(2,1)} copy(bf16[2,8,6,128]{3,1,2,0:T(8,128)(2,1)} %bitcast.3) | data formatting | bytes 49152

commit v2 on v1

--- a/solution.py
+++ b/solution.py
@@ -25,6 +25,22 @@
 
 def kernel(
     n,
+    pairs_hbm,
+    count_hbm,
+    parent_of_hbm,
+    octant_hbm,
+    src0_hbm,
+    disp0_hbm,
+    src1_hbm,
+    disp1_hbm,
+    currents,
+    near_blocks,
+    radiation,
+    trans0,
+    trans1,
+    phases,
+    interp,
+    out,
     pairs,
     count,
     parent_of,
@@ -33,14 +49,6 @@
     disp0,
     src1,
     disp1,
-    currents,
-    near_blocks,
-    radiation,
-    trans0,
-    trans1,
-    phases,
-    interp,
-    out,
     staged,
     pool,
     pool_turned,
@@ -86,24 +94,58 @@
     slot_count = pairs.shape[1]
     own_start = me * slots
 
+    barrier = pltpu.get_barrier_semaphore()
+    for step in range(1, n):
+        pl.semaphore_signal(
+            barrier, inc=1, device_id={"box": lax.rem(me + step, n)}, device_id_type=MESH
+        )
+    pl.semaphore_signal(barrier, inc=1, device_id={"sub": 1 - sub}, device_id_type=MESH)
+
     own_pool = pool.at[pl.ds(0, slots)]
     next_pool = pool.at[pl.ds(slots, slots)]
-    sources = (currents, radiation, phases, interp, trans1, near_blocks, trans0)
-    targets = (staged, rad, phase, interp_wide, table1, blocks, table0)
+    sources = (
+        currents,
+        radiation,
+        disp1_hbm,
+        src1_hbm,
+        trans1,
+        phases,
+        octant_hbm,
+        parent_of_hbm,
+        src0_hbm,
+        disp0_hbm,
+        pairs_hbm,
+        count_hbm,
+        interp,
+        trans0,
+        near_blocks,
+    )
+    targets = (
+        staged,
+        rad,
+        disp1,
+        src1,
+        table1,
+        phase,
+        octant,
+        parent_of,
+        src0,
+        disp0,
+        pairs,
+        count,
+        interp_wide,
+        table0,
+        blocks,
+    )
     local = [
         pltpu.make_async_copy(a, b, local_sem.at[i])
         for i, (a, b) in enumerate(zip(sources, targets))
     ]
     for copy in local:
         copy.start()
-    get_currents, get_rad, get_phase, get_interp, get_table1, get_blocks, get_table0 = local
-
-    barrier = pltpu.get_barrier_semaphore()
-    for step in range(1, n):
-        pl.semaphore_signal(
-            barrier, inc=1, device_id={"box": lax.rem(me + step, n)}, device_id_type=MESH
-        )
-    pl.semaphore_signal(barrier, inc=1, device_id={"sub": 1 - sub}, device_id_type=MESH)
+    get_currents, get_rad, *get_parent_lists = local[:5]
+    get_phase, *get_lists = local[5:12]
+    get_interp, get_table0, get_blocks = local[12:]
 
     get_currents.wait()
     for b in range(slots):
@@ -149,7 +191,8 @@
     def _():
         pool[pl.ds(slots, slots)] = jnp.zeros((slots,) + pool.shape[1:], BF16)
 
-    get_table1.wait()
+    for copy in get_parent_lists:
+        copy.wait()
     position = lax.broadcasted_iota(jnp.int32, (parents, table1.shape[2]), 0)
     own_operator = pl.ds(me * parents_here, parents_here)
     for r in range(parents_here):
@@ -184,6 +227,8 @@
 
     for b in range(slots, 2 * slots):
         pool_turned[b] = turned(pool[b].astype(F32)).astype(BF16)
+    for copy in get_lists:
+        copy.wait()
     get_blocks.wait()
 
     def near_step(p, carry):
@@ -387,15 +432,16 @@
     slot_count = near_pairs.shape[0]
     cut = unknowns // lax.axis_size("sub")
     per_box = jnp.transpose(currents, (0, 2, 1, 3))
-    scalars = pl.BlockSpec(memory_space=pltpu.SMEM)
-    away = pl.BlockSpec(memory_space=pl.ANY)
+    away = pl.BlockSpec(memory_space=pltpu.HBM)
+    lists = (near_pairs.T, near_count, parent_of, octant, far0_src, far0_disp, far1_src, far1_disp)
     dma = pltpu.SemaphoreType.DMA
     result = pl.pallas_call(
         functools.partial(kernel, n),
         out_shape=jax.ShapeDtypeStruct((2, slots, angles, cut), BF16),
-        in_specs=[scalars] * 8 + [away] * 7,
+        in_specs=[away] * 15,
         out_specs=pl.BlockSpec(memory_space=pltpu.VMEM),
-        scratch_shapes=[
+        scratch_shapes=[pltpu.SMEM(entry.shape, jnp.int32) for entry in lists]
+        + [
             pltpu.VMEM(per_box.shape, BF16),
             pltpu.VMEM((2 * slots, rows, unknowns), BF16),
             pltpu.VMEM((2 * slots, rows, unknowns), BF16),
@@ -418,7 +464,7 @@
             pltpu.VMEM((slots, rows, unknowns), BF16),
             pltpu.VMEM((slots, rows, cut), BF16),
             pltpu.VMEM((slots, rows, cut), BF16),
-            dma((7,)),
+            dma((15,)),
             dma((n - 1,)),
             dma((n - 1,)),
             dma((n - 1,)),
@@ -434,14 +480,7 @@
             collective_id=0, has_side_effects=True, vmem_limit_bytes=60 * 1024 * 1024
         ),
     )(
-        jnp.transpose(near_pairs),
-        near_count,
-        parent_of,
-        octant,
-        far0_src,
-        far0_disp,
-        far1_src,
-        far1_disp,
+        *lists,
         per_box,
         near_blocks,
         radiation,

time: 19 us -> 18.3 us (0.963)
  Pallas kernels: 16.8 us -> 16.1 us
    pallas_call x1, Pallas kernels: 16.8 us -> 16.1 us  [shards(): pl.pallas_call(functools.partial(kernel, n), out_shape=jax.ShapeDtypeStru...]
where the time goes in v2:
time: 18.3 us; the launch traced here: 18.1 us
  Pallas kernels  16.1 us (88%)
  local copies, waits for them, and re-layouts  1.35 us (7%)
  between operations  0.66 us (4%)
    pallas_call x1, Pallas kernels, shards(): pl.pallas_call(functools.partial(kernel, n), out_shape=jax.ShapeDtypeStru...  16.1 us
    unnamed x1, local copies, waits for them, and re-layouts  1.35 us

profile of v2, /device:TPU:0, one launch (start us, length us, event | category | flops | bytes accessed | tf_op | source)
XLA Modules:
  0.0 18.1 jit_solution(4712146760925316481)
XLA Ops:
  0.7 16.1 %shard_map.145 = bf16[2,6,8,128]{3,2,1,0:T(8,128)(2,1)} custom-call(s32[2,12]{1,0:T(2,128)} %bitcast.5, s32[1]{0:T(128)S(6)} %copy.17.count_hbm, s32[24]{0:T(128)} %parent_of_hbm.1, s32[24]{0:T(128)} %octant_hbm.1, s32[6,16]{1,0:T(8,128)} %src0_hbm.1, s32[6,16]{1,0:T(8,128)} %disp0_hbm.1, s32[2,8]{1,0:T(2,128)} %src1_hbm.1, s32[2,8]{1,0:T(2,128)} %disp1_hbm.1, ...), custom_call_target="tpu_custom_call" | custom-call | tf_op jit(solution)/shard_map/pallas_call | solution.py:438
  16.7 1.3 %copy.18 = bf16[2,8,6,128]{3,1,2,0:T(8,128)(2,1)} copy(bf16[2,8,6,128]{3,1,2,0:T(8,128)(2,1)} %bitcast.3) | data formatting | bytes 49152

commit v3 on v2

--- a/solution.py
+++ b/solution.py
@@ -50,6 +50,7 @@
     src1,
     disp1,
     staged,
+    mine,
     pool,
     pool_turned,
     blocks,
@@ -63,6 +64,7 @@
     pattern,
     operators,
     lifted,
+    down,
     parent,
     forward,
     backward,
@@ -101,7 +103,6 @@
         )
     pl.semaphore_signal(barrier, inc=1, device_id={"sub": 1 - sub}, device_id_type=MESH)
 
-    own_pool = pool.at[pl.ds(0, slots)]
     next_pool = pool.at[pl.ds(slots, slots)]
     sources = (
         currents,
@@ -141,7 +142,7 @@
         pltpu.make_async_copy(a, b, local_sem.at[i])
         for i, (a, b) in enumerate(zip(sources, targets))
     ]
-    for copy in local:
+    for copy in local[:-1]:
         copy.start()
     get_currents, get_rad, *get_parent_lists = local[:5]
     get_phase, *get_lists = local[5:12]
@@ -150,13 +151,15 @@
     get_currents.wait()
     for b in range(slots):
         wide = jnp.concatenate([staged[0, b].astype(F32), staged[1, b].astype(F32)], axis=0)
+        mine[b] = wide.astype(BF16)
         pool[b] = wide.astype(BF16)
         pool_turned[b] = turned(wide).astype(BF16)
     get_rad.wait()
+    get_blocks.start()
     own_box = pl.ds(own_start, slots)
     for b in range(slots):
         pattern[own_start + b] = (
-            dot(pool[b], rad[0, b, 0], 1) + dot(pool_turned[b], rad[1, b, 0], 1)
+            dot(mine[b], rad[0, b, 0], 1) + dot(pool_turned[b], rad[1, b, 0], 1)
         ).astype(BF16)
 
     pl.semaphore_wait(barrier, n)
@@ -175,7 +178,7 @@
         pattern_copies.append(copy)
 
     next_copy = pltpu.make_async_remote_copy(
-        src_ref=own_pool,
+        src_ref=mine,
         dst_ref=next_pool,
         send_sem=next_send,
         recv_sem=next_recv,
@@ -217,28 +220,16 @@
         copy.start()
         operator_copies.append(copy)
 
-    get_phase.wait()
-    cosine[...] = jnp.cos(phase[...])
-    sine[...] = jnp.sin(phase[...])
-
-    @pl.when(me < n - 1)
-    def _():
-        next_copy.wait_recv()
-
-    for b in range(slots, 2 * slots):
-        pool_turned[b] = turned(pool[b].astype(F32)).astype(BF16)
     for copy in get_lists:
         copy.wait()
     get_blocks.wait()
 
-    def near_step(p, carry):
-        source = jnp.clip(pairs[1, p] - own_start, 0, 2 * slots - 1)
+    def backward_step(p, carry):
         target = jnp.clip(pairs[0, p] - own_start, 0, slots - 1)
-        forward[p] = dot(pool[source], blocks[0, p], 1) + dot(pool_turned[source], blocks[1, p], 1)
-        backward[p] = dot(pool[target], blocks[0, p], 0) + dot(pool_turned[target], blocks[1, p], 0)
+        backward[p] = dot(mine[target], blocks[0, p], 0) + dot(pool_turned[target], blocks[1, p], 0)
         return carry
 
-    lax.fori_loop(0, slot_count, near_step, 0, unroll=True)
+    lax.fori_loop(0, slot_count, backward_step, 0, unroll=True)
 
     def mirror_weight(p, b):
         source = pairs[1, p]
@@ -276,6 +267,53 @@
     def _():
         mirror_in[...] = jnp.zeros(mirror_in.shape, BF16)
 
+    get_phase.wait()
+    cosine[...] = jnp.cos(phase[...])
+    sine[...] = jnp.sin(phase[...])
+    get_interp.wait()
+    narrow = interp_wide[...].astype(BF16)
+    parent[...] = jnp.zeros(parent.shape, F32)
+    merged = slots * rows
+
+    def lift_part(part):
+        start = part * slots
+        part_rows = pattern[pl.ds(start, slots)].reshape(merged, pattern.shape[2])
+        up = dot(part_rows, narrow, 1)
+        for i in range(slots):
+            cos_row = cosine[pl.ds(octant[start + i], 1), :]
+            sin_row = sine[pl.ds(octant[start + i], 1), :]
+            real = up[i * rows : i * rows + half_rows]
+            imag = up[i * rows + half_rows : (i + 1) * rows]
+            lifted[i] = jnp.concatenate(
+                [real * cos_row - imag * sin_row, real * sin_row + imag * cos_row], axis=0
+            )
+
+        def sum_parent(r, carry):
+            total = parent[r]
+            for i in range(slots):
+                weight = jnp.where(parent_of[start + i] == r, 1.0, 0.0).astype(F32)
+                total = total + weight * lifted[i]
+            parent[r] = total
+            return carry
+
+        lax.fori_loop(0, parents, sum_parent, 0, unroll=parents <= 8)
+
+    lift_part(me)
+
+    @pl.when(me < n - 1)
+    def _():
+        next_copy.wait_recv()
+
+    for b in range(slots, 2 * slots):
+        pool_turned[b] = turned(pool[b].astype(F32)).astype(BF16)
+
+    def forward_step(p, carry):
+        source = jnp.clip(pairs[1, p] - own_start, 0, 2 * slots - 1)
+        forward[p] = dot(pool[source], blocks[0, p], 1) + dot(pool_turned[source], blocks[1, p], 1)
+        return carry
+
+    lax.fori_loop(0, slot_count, forward_step, 0, unroll=True)
+
     def near_box(b, carry):
         def step(p, total):
             total = total + target_weight(p, b) * forward[p]
@@ -286,64 +324,25 @@
 
     lax.fori_loop(0, slots, near_box, 0)
 
-    get_interp.wait()
-    narrow = interp_wide[...].astype(BF16)
-    for copy in pattern_copies:
-        copy.wait_recv()
-
-    def lift_box(b, carry):
-        up = dot(pattern[b], narrow, 1)
-        cos_row = cosine[pl.ds(octant[b], 1), :]
-        sin_row = sine[pl.ds(octant[b], 1), :]
-        real, imag = up[:half_rows], up[half_rows:]
-        lifted[b] = jnp.concatenate(
-            [real * cos_row - imag * sin_row, real * sin_row + imag * cos_row], axis=0
-        )
-        return carry
-
-    def lift_some(part, carry):
-        return lax.fori_loop(
-            0, slots, lambda b, c: lift_box(part * slots + b, c), carry, unroll=True
-        )
-
-    lax.fori_loop(0, boxes // slots, lift_some, 0)
-
-    def sum_parent(r, carry):
-        def part_sum(part, total):
-            def step(i, total):
-                b = part * slots + i
-                weight = jnp.where(parent_of[b] == r, 1.0, 0.0).astype(F32)
-                return total + weight * lifted[b]
-
-            return lax.fori_loop(0, slots, step, total, unroll=True)
-
-        total = lax.fori_loop(0, boxes // slots, part_sum, zero)
-        parent[r] = total.astype(BF16).astype(F32)
-        return carry
-
-    lax.fori_loop(0, parents, sum_parent, 0)
+    for step in sorted(range(1, n), key=lambda k: min(k, n - k)):
+        pattern_copies[step - 1].wait_recv()
+        lift_part(lax.rem(me + n - step, n))
 
     for copy in operator_copies:
         copy.wait_recv()
     get_table0.wait()
 
-    def far_box(b, carry):
-        quarter = jnp.zeros((half_rows, pattern.shape[2]), F32)
-
-        def translate(k, total):
-            value = pattern[src0[b, k]].astype(F32)
-            factor = table0[disp0[b, k]].astype(F32)
-            real, imag = value[:half_rows], value[half_rows:]
-            fr, fi = factor[0:1], factor[1:2]
-            return (total[0] + (real * fr - imag * fi), total[1] + (real * fi + imag * fr))
-
-        far_real, far_imag = lax.fori_loop(
-            0, src0.shape[1], translate, (quarter, quarter), unroll=True
-        )
+    def round_parent(r, carry):
+        parent[r] = parent[r].astype(BF16).astype(F32)
+        return carry
+
+    lax.fori_loop(0, parents, round_parent, 0, unroll=parents <= 8)
+
+    for b in range(slots):
         owner = parent_of[own_start + b]
-        operator = operators[owner].astype(F32)
         pf_real = jnp.zeros((half_rows, parent.shape[2]), F32)
         pf_imag = jnp.zeros((half_rows, parent.shape[2]), F32)
+        operator = operators[owner].astype(F32)
         for s in range(parents):
             value = parent[s]
             real, imag = value[:half_rows], value[half_rows:]
@@ -356,16 +355,28 @@
         spot = octant[own_start + b]
         cos_row = cosine[pl.ds(spot, 1), :]
         sin_row = sine[pl.ds(spot, 1), :]
-        down = jnp.concatenate(
+        down[b] = jnp.concatenate(
             [pf_real * cos_row + pf_imag * sin_row, pf_imag * cos_row - pf_real * sin_row], axis=0
         ).astype(BF16)
-        field = jnp.concatenate([far_real, far_imag], axis=0) + dot(down, narrow, 0)
+    descended = dot(down[...].reshape(merged, down.shape[2]), narrow, 0)
+
+    quarter = jnp.zeros((half_rows, pattern.shape[2]), F32)
+    for b in range(slots):
+
+        def translate(k, total):
+            value = pattern[src0[b, k]].astype(F32)
+            factor = table0[disp0[b, k]].astype(F32)
+            real, imag = value[:half_rows], value[half_rows:]
+            fr, fi = factor[0:1], factor[1:2]
+            return (total[0] + (real * fr - imag * fi), total[1] + (real * fi + imag * fr))
+
+        far_real, far_imag = lax.fori_loop(
+            0, src0.shape[1], translate, (quarter, quarter), unroll=True
+        )
+        field = jnp.concatenate([far_real, far_imag], axis=0) + descended[b * rows : (b + 1) * rows]
         field = field.astype(BF16)
         wide = turned(field.astype(F32)).astype(BF16)
         near_sum[b] += dot(field, rad[0, b, 0], 0) + dot(wide, rad[1, b, 0], 0)
-        return carry
-
-    lax.fori_loop(0, slots, far_box, 0)
 
     @pl.when(me > 0)
     def _():
@@ -443,6 +454,7 @@
         scratch_shapes=[pltpu.SMEM(entry.shape, jnp.int32) for entry in lists]
         + [
             pltpu.VMEM(per_box.shape, BF16),
+            pltpu.VMEM((slots, rows, unknowns), BF16),
             pltpu.VMEM((2 * slots, rows, unknowns), BF16),
             pltpu.VMEM((2 * slots, rows, unknowns), BF16),
             pltpu.VMEM(near_blocks.shape, BF16),
@@ -455,7 +467,8 @@
             pltpu.VMEM(interp.shape, F32),
             pltpu.VMEM((boxes, rows, fine), BF16),
             pltpu.VMEM((parents, 2 * parents, coarse), BF16),
-            pltpu.VMEM((boxes, rows, coarse), F32),
+            pltpu.VMEM((slots, rows, coarse), F32),
+            pltpu.VMEM((slots, rows, coarse), BF16),
             pltpu.VMEM((parents, rows, coarse), F32),
             pltpu.VMEM((slot_count, rows, unknowns), F32),
             pltpu.VMEM((slot_count, rows, unknowns), F32),

time: 18.3 us -> 15.5 us (0.85)
  Pallas kernels: 16.1 us -> 13.3 us
    pallas_call x1, Pallas kernels: 16.1 us -> 13.3 us  [shards(): pl.pallas_call(functools.partial(kernel, n), out_shape=jax.ShapeDtypeStru...]
where the time goes in v3:
time: 15.5 us; the launch traced here: 15.3 us
  Pallas kernels  13.3 us (86%)
  local copies, waits for them, and re-layouts  1.35 us (9%)
  between operations  0.66 us (4%)
    pallas_call x1, Pallas kernels, shards(): pl.pallas_call(functools.partial(kernel, n), out_shape=jax.ShapeDtypeStru...  13.3 us
    unnamed x1, local copies, waits for them, and re-layouts  1.35 us

profile of v3, /device:TPU:0, one launch (start us, length us, event | category | flops | bytes accessed | tf_op | source)
XLA Modules:
  0.0 15.3 jit_solution(2487956484589833037)
XLA Ops:
  0.7 13.3 %shard_map.145 = bf16[2,6,8,128]{3,2,1,0:T(8,128)(2,1)} custom-call(s32[2,12]{1,0:T(2,128)} %bitcast.5, s32[1]{0:T(128)S(6)} %copy.17.count_hbm, s32[24]{0:T(128)} %parent_of_hbm.1, s32[24]{0:T(128)} %octant_hbm.1, s32[6,16]{1,0:T(8,128)} %src0_hbm.1, s32[6,16]{1,0:T(8,128)} %disp0_hbm.1, s32[2,8]{1,0:T(2,128)} %src1_hbm.1, s32[2,8]{1,0:T(2,128)} %disp1_hbm.1, ...), custom_call_target="tpu_custom_call" | custom-call | tf_op jit(solution)/shard_map/pallas_call | solution.py:449
  13.9 1.3 %copy.18 = bf16[2,8,6,128]{3,1,2,0:T(8,128)(2,1)} copy(bf16[2,8,6,128]{3,1,2,0:T(8,128)(2,1)} %bitcast.3) | data formatting | bytes 49152

commit v4 on v3

--- a/solution.py
+++ b/solution.py
@@ -249,7 +249,7 @@
         mirror_out[b] = lax.fori_loop(0, slot_count, step, zero, unroll=True).astype(BF16)
         return carry
 
-    lax.fori_loop(0, slots, mirror_box, 0)
+    lax.fori_loop(0, slots, mirror_box, 0, unroll=True)
     mirror_copy = pltpu.make_async_remote_copy(
         src_ref=mirror_out,
         dst_ref=mirror_in,
@@ -322,7 +322,7 @@
         near_sum[b] = lax.fori_loop(0, slot_count, step, zero, unroll=True)
         return carry
 
-    lax.fori_loop(0, slots, near_box, 0)
+    lax.fori_loop(0, slots, near_box, 0, unroll=True)
 
     for step in sorted(range(1, n), key=lambda k: min(k, n - k)):
         pattern_copies[step - 1].wait_recv()

time: 15.5 us -> 15.2 us (0.981)
  Pallas kernels: 13.3 us -> 13 us
    pallas_call x1, Pallas kernels: 13.3 us -> 13 us  [shards(): pl.pallas_call(functools.partial(kernel, n), out_shape=jax.ShapeDtypeStru...]
where the time goes in v4:
time: 15.2 us; the launch traced here: 15 us
  Pallas kernels  13 us (86%)
  local copies, waits for them, and re-layouts  1.35 us (9%)
  between operations  0.66 us (4%)
    pallas_call x1, Pallas kernels, shards(): pl.pallas_call(functools.partial(kernel, n), out_shape=jax.ShapeDtypeStru...  13 us
    unnamed x1, local copies, waits for them, and re-layouts  1.35 us

profile of v4, /device:TPU:0, one launch (start us, length us, event | category | flops | bytes accessed | tf_op | source)
XLA Modules:
  0.0 15.0 jit_solution(12032990974234649622)
XLA Ops:
  0.7 13.0 %shard_map.145 = bf16[2,6,8,128]{3,2,1,0:T(8,128)(2,1)} custom-call(s32[2,12]{1,0:T(2,128)} %bitcast.5, s32[1]{0:T(128)S(6)} %copy.17.count_hbm, s32[24]{0:T(128)} %parent_of_hbm.1, s32[24]{0:T(128)} %octant_hbm.1, s32[6,16]{1,0:T(8,128)} %src0_hbm.1, s32[6,16]{1,0:T(8,128)} %disp0_hbm.1, s32[2,8]{1,0:T(2,128)} %src1_hbm.1, s32[2,8]{1,0:T(2,128)} %disp1_hbm.1, ...), custom_call_target="tpu_custom_call" | custom-call | tf_op jit(solution)/shard_map/pallas_call | solution.py:449
  13.6 1.3 %copy.18 = bf16[2,8,6,128]{3,1,2,0:T(8,128)(2,1)} copy(bf16[2,8,6,128]{3,1,2,0:T(8,128)(2,1)} %bitcast.3) | data formatting | bytes 49152
